TPU v7x, 256 devices: a whole 4x4x8 slice. The times are simulated.
256 devices in a mesh: energy: 32 (over z, y_lo, core), cell: 8 (over x, y_hi).
Axes of the slice: x: 4, y: 4 (y_hi: 2, y_lo: 2; y = y_hi * 2 + y_lo), z: 8, core: 2. Of those that a mesh axis runs over, the one named last changes fastest.
Arguments:
- glesser: float32 [16, 128, 2, 9216], P('cell', 'energy'), may hold values from -4 to 4, as said below
- wlesser: float32 [16, 128, 2, 9216], P('cell', 'energy'), may hold values from -4 to 4, as said below
- gret_diag: float32 [16, 128, 2, 9216], P('cell', 'energy'), may hold values from -0.4375 to 0.4375
- gret_upper: float32 [16, 128, 2, 9216], P('cell', 'energy'), may hold values from -0.4375 to 0.4375
Outputs:
- sigma_lesser: float32 [16, 128, 2, 9216], P('cell', 'energy')
- g_lesser_new: float32 [16, 128, 2, 9216], P('cell', 'energy')
Inputs may be any that keep to these rules, and one draw needn't show every extreme that they name: Each block of glesser is anti-Hermitian: its real part is antisymmetric and its imaginary part symmetric. Each block of wlesser is anti-Hermitian: its real part is antisymmetric and its imaginary part symmetric.
All inputs are finite; a program needn't handle non-finite values.
Results may differ from a plain program's by a relative error of at most 0.000098.
Values sent between devices are 32-bit elements; how exact they have to be, the bound alone decides.
A program may use at most 128 MiB of HBM per device.

v0:
```python
import functools

import jax
import jax.numpy as jnp
import ml_dtypes
import numpy as np
from jax import lax
from jax.experimental import pallas as pl
from jax.experimental.pallas import tpu as pltpu
from jax.sharding import PartitionSpec as P

MESH = pl.DeviceIdType.MESH
B = 96
NE = 128
PEERS = 32
HALF = 36
F32 = jnp.float32
BF16 = jnp.bfloat16
VMEM_LIMIT = 56 * 1024 * 1024


def two_terms(x):
    high = x.astype(ml_dtypes.bfloat16)
    return high, (x - high.astype(np.float64)).astype(ml_dtypes.bfloat16)


def transforms():
    n = np.arange(NE)
    k = np.arange(NE)
    angle = 2.0 * np.pi / (4 * NE) * ((n[None, :] * (1 - 4 * k[:, None])) % (4 * NE))
    forward = np.zeros((2, 2, NE, NE, 2))
    inverse = np.zeros((NE, 2, 2, 2, NE))
    scale = NE ** -0.5 / NE
    for part in range(2):
        forward[part, 0, :, :, part] = np.cos(angle)
        forward[part, 1, :, :, part] = np.sin(angle)
        inverse[:, part, part, 0, :] = np.cos(angle).T * scale
        inverse[:, part, part, 1, :] = np.sin(angle).T * scale
    return forward.reshape(512, 256), inverse.reshape(256, 512)


def split(x):
    high = x.astype(BF16)
    return high, (x - high.astype(F32)).astype(BF16)


def dot3(ah, al, bh, bl, dims=(((1,), (0,)), ((), ()))):
    d = functools.partial(lax.dot_general, dimension_numbers=dims, preferred_element_type=F32)
    return d(ah, bh) + (d(al, bh) + d(ah, bl))


def whole(ref, sem):
    return pltpu.make_async_copy(ref, ref, sem)


def exchange_kernel(
    g_hbm, w_hbm, u_hbm, fh, fl, ih, il,
    sg, above, below, ub,
    gv, wv, pk, rv, ob,
    load_sem, self_sem, send_sem, xsend_sem, recv_sem, back_sem, xback_sem, sig_sem, hop_send, hop_recv,
):
    me = lax.axis_index("energy")
    k = lax.axis_index("cell")
    my_z = me // 4
    my_i = my_z // 2
    my_c = my_z % 2
    is_extra = jnp.equal(me % 4, my_i)
    has_up = k < 7
    has_down = k > 0

    for c in range(2):
        pltpu.make_async_copy(g_hbm.at[pl.ds(4 * c, 4)], gv.at[pl.ds(4 * c, 4), pl.ds(0, 144)], load_sem.at[c, 0]).start()
        pltpu.make_async_copy(w_hbm.at[pl.ds(4 * c, 4)], wv.at[pl.ds(4 * c, 4), pl.ds(0, 144)], load_sem.at[c, 1]).start()

    barrier = pltpu.get_barrier_semaphore()

    def greet(i, carry):
        pl.semaphore_signal(barrier, inc=1, device_id={"energy": lax.rem(me + i, PEERS)}, device_id_type=MESH)
        return carry

    lax.fori_loop(1, PEERS, greet, 0)

    @pl.when(has_up)
    def _():
        pl.semaphore_signal(barrier, inc=1, device_id={"cell": k + 1}, device_id_type=MESH)

    @pl.when(has_down)
    def _():
        pl.semaphore_signal(barrier, inc=1, device_id={"cell": k - 1}, device_id_type=MESH)

    row = lax.broadcasted_iota(jnp.int32, (40, 128), 0)
    lane = lax.broadcasted_iota(jnp.int32, (40, 128), 1)
    slot_index = row * 128 + lane
    a_index = (slot_index * 43691) >> 22
    b_index = slot_index - a_index * B
    direct = b_index >= a_index
    diagonal = b_index == a_index
    near = lane >= 48

    def pack(c):
        for which, source in enumerate((gv, wv)):
            pltpu.make_async_copy(
                (g_hbm, w_hbm)[which].at[pl.ds(4 * c, 4)], source.at[pl.ds(4 * c, 4), pl.ds(0, 144)], load_sem.at[c, which]
            ).wait()

            def one(e, carry):
                blk = 4 * c + e
                first, far = [], []
                for part in range(2):
                    first.append(source[blk, pl.ds(part, 40, stride=2), :])
                    here = source[blk, pl.ds(72 + part, 40, stride=2), :]
                    after = source[blk, pl.ds(74 + part, 40, stride=2), :]
                    far.append(pltpu.roll(jnp.where(near, here, after), 80, 1))
                re = jnp.where(direct, first[0], far[0])
                re = jnp.where(diagonal, far[1], re)
                im = jnp.where(direct, first[1], far[1])
                base = which * 8 + 2 * e
                pk[c, pl.ds(base, 40, stride=16), :] = re
                pk[c, pl.ds(base + 1, 40, stride=16), :] = im
                return carry

            lax.fori_loop(0, 4, one, 0)

    def outgoing(c, p):
        return pltpu.make_async_remote_copy(
            src_ref=pk.at[c, pl.ds(p * 16, 16)], dst_ref=rv.at[c, me], send_sem=send_sem.at[c], recv_sem=recv_sem.at[c],
            device_id={"energy": p}, device_id_type=MESH,
        )

    def extra_out(c, i):
        return pltpu.make_async_remote_copy(
            src_ref=pk.at[c, pl.ds((PEERS + i) * 16, 16)], dst_ref=rv.at[2, me], send_sem=xsend_sem.at[c, i],
            recv_sem=recv_sem.at[2], device_id={"energy": 4 * (2 * i + c) + i}, device_id_type=MESH,
        )

    def send(c):
        def start(i, carry):
            outgoing(c, lax.rem(me + i, PEERS)).start()
            return carry

        pltpu.make_async_copy(pk.at[c, pl.ds(me * 16, 16)], rv.at[c, me], recv_sem.at[c]).start()
        lax.fori_loop(1, PEERS, start, 0)
        for i in range(4):
            mine = jnp.equal(me, 4 * (2 * i + c) + i)

            @pl.when(jnp.logical_not(mine))
            def _(i=i):
                extra_out(c, i).start()

            @pl.when(mine)
            def _(i=i):
                pltpu.make_async_copy(pk.at[c, pl.ds((PEERS + i) * 16, 16)], rv.at[2, me], recv_sem.at[2]).start()

    pack(0)
    pl.semaphore_wait(barrier, 31 + has_up.astype(jnp.int32) + has_down.astype(jnp.int32))
    send(0)
    pack(1)
    send(1)

    def u_copy():
        return pltpu.make_async_remote_copy(
            src_ref=u_hbm.at[pl.ds(4, 4)], dst_ref=ub, send_sem=hop_send.at[0], recv_sem=hop_recv.at[0],
            device_id={"cell": k + 1}, device_id_type=MESH,
        )

    def down_copy():
        return pltpu.make_async_remote_copy(
            src_ref=sg.at[0], dst_ref=above, send_sem=hop_send.at[1], recv_sem=hop_recv.at[1],
            device_id={"cell": k - 1}, device_id_type=MESH,
        )

    def up_copy():
        return pltpu.make_async_remote_copy(
            src_ref=sg.at[1], dst_ref=below, send_sem=hop_send.at[2], recv_sem=hop_recv.at[2],
            device_id={"cell": k + 1}, device_id_type=MESH,
        )

    @pl.when(has_up)
    def _():
        u_copy().start()

    @pl.when(jnp.logical_not(has_up))
    def _():
        above[...] = jnp.zeros_like(above)

    @pl.when(jnp.logical_not(has_down))
    def _():
        below[...] = jnp.zeros_like(below)
        ub[...] = jnp.zeros_like(ub)

    def back(slot, c, tile, p):
        return pltpu.make_async_remote_copy(
            src_ref=ob.at[slot, p], dst_ref=sg.at[c, tile], send_sem=back_sem.at[slot], recv_sem=sig_sem.at[c],
            device_id={"energy": p}, device_id_type=MESH,
        )

    def convolve(slot, c, tile):
        whole(rv.at[slot], recv_sem.at[slot]).wait()
        green = rv[slot, :, 0:8, :].reshape(256, 128)
        screen = rv[slot, :, 8:16, :].reshape(256, 128)
        xh, xl = split(jnp.concatenate([green, screen], 1))
        hat = dot3(fh[...], fl[...], xh, xl)
        xr, xi, yr, yi = (hat[128 * j:128 * j + 128] for j in range(4))
        xrg, xrw, xig, xiw = xr[:, :128], xr[:, 128:], xi[:, :128], xi[:, 128:]
        yrg, yrw, yig, yiw = yr[:, :128], yr[:, 128:], yi[:, :128], yi[:, 128:]
        xx_r = xrg * xrw - xig * xiw
        xx_i = xrg * xiw + xig * xrw
        yy_r = yrg * yrw - yig * yiw
        yy_i = yrg * yiw + yig * yrw
        xy_r = (xrg * yrw - xig * yiw) + (yrg * xrw - yig * xiw)
        xy_i = (xrg * yiw + xig * yrw) + (yrg * xiw + yig * xrw)
        main = jnp.concatenate([-xy_r, -xy_i, xx_r - yy_r, xx_i - yy_i], 0)
        diag = jnp.concatenate([-xx_r, -xx_i, -yy_r, -yy_i], 0)
        zh, zl = split(jnp.concatenate([main, diag], 1))
        out = dot3(ih[...], il[...], zh, zl)
        position = tile * 128 + lax.broadcasted_iota(jnp.int32, (256, 128), 1)
        on_diagonal = position == ((position * 43241) >> 22) * 97
        ob[slot] = jnp.where(on_diagonal, out[:, 128:], out[:, :128]).reshape(PEERS, 8, 128)

        pltpu.make_async_copy(ob.at[slot, me], sg.at[c, tile], sig_sem.at[c]).start()

        def start(i, carry):
            back(slot, c, tile, lax.rem(me + i, PEERS)).start()
            return carry

        lax.fori_loop(1, PEERS, start, 0)

    def phase(c, carry):
        def step(j, inner):
            slot = jnp.where(j == 0, c, 2)
            tile = jnp.where(j == 0, me, PEERS + my_i)
            convolve(slot, c, tile)
            return inner

        count = 1 + jnp.where(jnp.logical_and(is_extra, my_c == c), 1, 0)
        lax.fori_loop(0, count, step, 0)
        return carry

    lax.fori_loop(0, 2, phase, 0)

    whole(sg.at[0], sig_sem.at[0]).wait()

    @pl.when(has_down)
    def _():
        down_copy().start()

    whole(sg.at[1], sig_sem.at[1]).wait()

    @pl.when(has_up)
    def _():
        up_copy().start()

    for c in range(2):
        whole(pk.at[c, pl.ds(0, 31 * 16)], send_sem.at[c]).wait()
        for i in range(4):
            @pl.when(jnp.logical_not(jnp.equal(me, 4 * (2 * i + c) + i)))
            def _(c=c, i=i):
                extra_out(c, i).wait_send()
        whole(ob.at[c, pl.ds(0, 31)], back_sem.at[c]).wait()

    @pl.when(is_extra)
    def _():
        whole(ob.at[2, pl.ds(0, 31)], back_sem.at[2]).wait()

    @pl.when(has_up)
    def _():
        u_copy().wait_send()
        up_copy().wait_send()
        down_copy().wait_recv()

    @pl.when(has_down)
    def _():
        down_copy().wait_send()
        u_copy().wait_recv()
        up_copy().wait_recv()


def update_kernel(
    sg, above, below, ub, rd, ru,
    sig_out, new_out,
    km, sf, es_h, es_l, el_h, el_l,
):
    row48 = lax.broadcasted_iota(jnp.int32, (48, 128), 0)
    lane48 = lax.broadcasted_iota(jnp.int32, (48, 128), 1)
    lane8 = lax.broadcasted_iota(jnp.int32, (8, 128), 1)
    lane24 = lax.broadcasted_iota(jnp.int32, (24, 128), 1)
    zero48 = jnp.zeros((80, 128), F32)
    zero32 = jnp.zeros((32, 128), F32)
    inside48 = lane48 < B

    def to_rows(u0, u1, u2, lane):
        r1 = jnp.where(lane < 32, pltpu.roll(u0, 32, 1), pltpu.roll(u1, 32, 1))
        r2 = jnp.where(lane < 64, pltpu.roll(u1, 64, 1), pltpu.roll(u2, 64, 1))
        return u0, r1, r2, pltpu.roll(u2, 96, 1)

    def to_tiles(r0, r1, r2, r3, lane):
        m1, m2, m3 = pltpu.roll(r1, 96, 1), pltpu.roll(r2, 64, 1), pltpu.roll(r3, 32, 1)
        return jnp.where(lane < 96, r0, m1), jnp.where(lane < 64, m1, m2), jnp.where(lane < 32, m2, m3)

    def store_pair(high, low, index, re, im):
        re = jnp.concatenate([re, zero32], 0)
        im = jnp.concatenate([im, zero32], 0)
        rh, rl = split(re)
        mh, ml = split(im)
        for ref, r, m in ((high, rh, mh), (low, rl, ml)):
            ref[index, 0:128, 0:128] = r
            ref[index, 0:128, 128:256] = m
            ref[index, 128:256, 0:128] = -m
            ref[index, 128:256, 128:256] = r

    for array in range(4):
        def take(t, array=array):
            return sg[array, t] if array < 2 else (above[t] if array == 2 else below[t])

        def rows(q, carry, array=array, take=take):
            for j, r in enumerate(to_rows(take(3 * q), take(3 * q + 1), take(3 * q + 2), lane8)):
                km[pl.ds(array * 384 + 4 * q + j, 8, stride=48), :] = r
            return carry

        lax.fori_loop(0, 12, rows, 0)

    def flat_store(re, im, out, blk):
        for part, x in ((0, re), (1, im)):
            sf[part] = x
        for part in range(2):
            tiles = to_tiles(*(sf[part, pl.ds(j, 24, stride=4), :] for j in range(4)), lane24)
            for j in range(3):
                out[blk, pl.ds(2 * j + part, 24, stride=6), :] = tiles[j]

    def unpack(index, carry):
        array = index // 4
        e = index % 4
        base = array * 384 + 2 * e * 48
        kr = km[pl.ds(pl.multiple_of(base, 8), 48), :]
        ki = km[pl.ds(pl.multiple_of(base + 48, 8), 48), :]
        krt = -jnp.concatenate([kr, zero48], 0).T
        kit = jnp.concatenate([ki, zero48], 0).T
        less, same = lane48 < row48, lane48 == row48
        top_r = jnp.where(less, krt[:48], jnp.where(same, 0.0, kr))
        top_i = jnp.where(less, kit[:48], ki)
        in_r = jnp.where(less, kr, jnp.where(same, 0.0, krt[:48]))
        in_i = jnp.where(less, ki, jnp.where(same, kr, kit[:48]))
        low_r = jnp.where(lane48 < 48, krt[48:96], pltpu.roll(in_r, 48, 1))
        low_i = jnp.where(lane48 < 48, kit[48:96], pltpu.roll(in_i, 48, 1))
        re = jnp.concatenate([jnp.where(inside48, top_r, 0.0), jnp.where(inside48, low_r, 0.0)], 0)
        im = jnp.concatenate([jnp.where(inside48, top_i, 0.0), jnp.where(inside48, low_i, 0.0)], 0)
        store_pair(es_h, es_l, index, re, im)

        @pl.when(index < 8)
        def _():
            flat_store(re, im, sig_out, index)

        return carry

    lax.fori_loop(0, 16, unpack, 0)

    lane96 = lax.broadcasted_iota(jnp.int32, (96, 128), 1)

    def matrix(source, blk, part):
        u = [source[blk, pl.ds(2 * j + part, 24, stride=6), :] for j in range(3)]
        for j, r in enumerate(to_rows(*u, lane24)):
            sf[part, pl.ds(j, 24, stride=4), :] = r
        return jnp.where(lane96 < B, sf[part], 0.0)

    def flip(x):
        return jnp.concatenate([x, zero32], 0).T[:96]

    def diag_prep(blk, carry):
        store_pair(el_h, el_l, blk, matrix(rd, blk, 0), matrix(rd, blk, 1))
        return carry

    def upper_prep(blk, carry):
        re, im = matrix(ru, blk, 0), matrix(ru, blk, 1)
        store_pair(el_h, el_l, 8 + blk, re, im)

        @pl.when(blk < 4)
        def _():
            store_pair(el_h, el_l, 20 + blk, flip(re), flip(im))

        return carry

    def below_prep(blk, carry):
        store_pair(el_h, el_l, 16 + blk, flip(matrix(ub, blk, 0)), flip(matrix(ub, blk, 1)))
        return carry

    lax.fori_loop(0, 8, diag_prep, 0)
    lax.fori_loop(0, 8, upper_prep, 0)
    lax.fori_loop(0, 4, below_prep, 0)

    transposed = (((1,), (1,)), ((), ()))

    def term(left, middle):
        x = dot3(el_h[left, 0:96, :], el_l[left, 0:96, :], es_h[middle], es_l[middle])
        xh, xl = split(x)
        return dot3(xh, xl, el_h[left], el_l[left], transposed)

    def combine(blk, carry):
        c = blk // 4
        e = blk % 4
        low = jnp.where(c == 0, 12 + e, e)
        high = jnp.where(c == 0, 4 + e, 8 + e)
        total = term(blk, blk) + term(16 + blk, low) + term(8 + blk, high)
        flat_store(total[:, :128], total[:, 128:], new_out, blk)
        return carry

    lax.fori_loop(0, 8, combine, 0)


def flat_view(x):
    return x.reshape(8, 2, 72, 128).transpose(0, 2, 1, 3).reshape(8, 144, 128)


def from_flat(y):
    return y.reshape(8, 72, 2, 128).transpose(0, 2, 1, 3).reshape(2, 4, 2, B * B)


def shards(glesser, wlesser, gret_diag, gret_upper):
    g, w, rd, ru = (flat_view(x) for x in (glesser, wlesser, gret_diag, gret_upper))
    forward, inverse = transforms()
    constants = [jnp.asarray(x) for x in (*two_terms(forward), *two_terms(inverse))]
    vmem = pl.BlockSpec(memory_space=pltpu.VMEM)
    hbm = pl.BlockSpec(memory_space=pl.ANY)
    dma = pltpu.SemaphoreType.DMA
    sg, above, below, ub = pl.pallas_call(
        exchange_kernel,
        out_shape=[
            jax.ShapeDtypeStruct((2, HALF, 8, 128), F32),
            jax.ShapeDtypeStruct((HALF, 8, 128), F32),
            jax.ShapeDtypeStruct((HALF, 8, 128), F32),
            jax.ShapeDtypeStruct((4, 144, 128), F32),
        ],
        in_specs=[hbm] * 3 + [vmem] * 4,
        out_specs=[vmem] * 4,
        scratch_shapes=[
            pltpu.VMEM((8, 160, 128), F32),
            pltpu.VMEM((8, 160, 128), F32),
            pltpu.VMEM((2, 640, 128), F32),
            pltpu.VMEM((3, PEERS, 16, 128), F32),
            pltpu.VMEM((3, PEERS, 8, 128), F32),
            dma((2, 2)), dma((2,)), dma((2,)), dma((2, 4)), dma((3,)), dma((3,)), dma((2,)), dma((2,)), dma((3,)), dma((3,)),
        ],
        compiler_params=pltpu.CompilerParams(collective_id=0, has_side_effects=True, vmem_limit_bytes=VMEM_LIMIT),
        name="exchange",
    )(g, w, ru, *constants)
    sigma, new = pl.pallas_call(
        update_kernel,
        out_shape=[jax.ShapeDtypeStruct((8, 144, 128), F32)] * 2,
        in_specs=[vmem] * 6,
        out_specs=[vmem] * 2,
        scratch_shapes=[
            pltpu.VMEM((4 * 384, 128), F32),
            pltpu.VMEM((2, 96, 128), F32),
            pltpu.VMEM((16, 256, 256), BF16),
            pltpu.VMEM((16, 256, 256), BF16),
            pltpu.VMEM((24, 256, 256), BF16),
            pltpu.VMEM((24, 256, 256), BF16),
        ],
        compiler_params=pltpu.CompilerParams(vmem_limit_bytes=VMEM_LIMIT),
        name="update",
    )(sg, above, below, ub, rd, ru)
    return from_flat(sigma), from_flat(new)


def solution(mesh):
    spec = P("cell", "energy", None, None)
    return jax.shard_map(shards, mesh=mesh, in_specs=(spec,) * 4, out_specs=(spec,) * 2, check_vma=False)
```

profile of v0, /device:TPU:4, one launch (start us, length us, event | category | flops | bytes accessed | tf_op | source)
XLA Modules:
  0.0 63.9 jit_solution(16955414552826771856)
XLA Ops:
  0.6 42.0 %exchange.1 = (f32[2,36,8,128]{3,2,1,0:T(8,128)}, f32[36,8,128]{2,1,0:T(8,128)}, f32[36,8,128]{2,1,0:T(8,128)}, f32[4,144,128]{2,1,0:T(8,128)}) custom-call(f32[8,144,128]{2,1,0:T(8,128)} %bitcast.32, f32[8,144,128]{2,1,0:T(8,128)} %bitcast.33, f32[8,144,128]{2,1,0:T(8,128)} %bitcast.30, bf16[512,256]{1,0:T(8,128)(2,1)} %constant.8.clone.fh, ...), custom_call_target="tpu_custom_call" | custom-call | tf_op jit(solution)/shard_map/exchange/pallas_call | solution.py:424
  42.6 21.2 %update.1 = (f32[8,144,128]{2,1,0:T(8,128)}, f32[8,144,128]{2,1,0:T(8,128)}) custom-call(f32[2,36,8,128]{3,2,1,0:T(8,128)} %get-tuple-element.8.sg, f32[36,8,128]{2,1,0:T(8,128)} %get-tuple-element.9.above, f32[36,8,128]{2,1,0:T(8,128)} %get-tuple-element.10.below, f32[4,144,128]{2,1,0:T(8,128)} %get-tuple-element.11.ub, f32[8,144,128]{2,1,0:T(8,128)} %bitcast.34, ...), custom_call_target="tpu_custom_call" | custom-call | tf_op jit(solution)/shard_map/update/pallas_call | solution.py:445
where the time goes:
time: 64.1 us; the launch traced here: 63.9 us
  Pallas kernels  63.2 us (99%)
    pallas_call x1, Pallas kernels, shards(): pl.pallas_call(exchange_kernel, out_shape=[jax.ShapeDtypeStruct((2, HALF,...  42 us
    pallas_call x1, Pallas kernels, shards(): pl.pallas_call(update_kernel, out_shape=[jax.ShapeDtypeStruct((8, 144, 12...  21.2 us

commit v1 on v0

--- a/solution.py
+++ b/solution.py
@@ -53,11 +53,11 @@
     return pltpu.make_async_copy(ref, ref, sem)
 
 
-def exchange_kernel(
-    g_hbm, w_hbm, u_hbm, fh, fl, ih, il,
-    sg, above, below, ub,
-    gv, wv, pk, rv, ob,
-    load_sem, self_sem, send_sem, xsend_sem, recv_sem, back_sem, xback_sem, sig_sem, hop_send, hop_recv,
+def kernel(
+    g_hbm, w_hbm, rd_hbm, u_hbm, fh, fl, ih, il,
+    sig_out, new_out,
+    gv, wv, pk, rv, ob, sg, above, below, ub, rd, ru, km, sf, es_h, es_l, el_h, el_l, total,
+    load_sem, ret_sem, send_sem, xsend_sem, recv_sem, back_sem, sig_sem, hop_send, hop_recv,
 ):
     me = lax.axis_index("energy")
     k = lax.axis_index("cell")
@@ -71,6 +71,11 @@
     for c in range(2):
         pltpu.make_async_copy(g_hbm.at[pl.ds(4 * c, 4)], gv.at[pl.ds(4 * c, 4), pl.ds(0, 144)], load_sem.at[c, 0]).start()
         pltpu.make_async_copy(w_hbm.at[pl.ds(4 * c, 4)], wv.at[pl.ds(4 * c, 4), pl.ds(0, 144)], load_sem.at[c, 1]).start()
+
+    load_rd = pltpu.make_async_copy(rd_hbm, rd, ret_sem.at[0])
+    load_ru = pltpu.make_async_copy(u_hbm, ru, ret_sem.at[1])
+    load_rd.start()
+    load_ru.start()
 
     barrier = pltpu.get_barrier_semaphore()
 
@@ -225,61 +230,6 @@
 
         lax.fori_loop(1, PEERS, start, 0)
 
-    def phase(c, carry):
-        def step(j, inner):
-            slot = jnp.where(j == 0, c, 2)
-            tile = jnp.where(j == 0, me, PEERS + my_i)
-            convolve(slot, c, tile)
-            return inner
-
-        count = 1 + jnp.where(jnp.logical_and(is_extra, my_c == c), 1, 0)
-        lax.fori_loop(0, count, step, 0)
-        return carry
-
-    lax.fori_loop(0, 2, phase, 0)
-
-    whole(sg.at[0], sig_sem.at[0]).wait()
-
-    @pl.when(has_down)
-    def _():
-        down_copy().start()
-
-    whole(sg.at[1], sig_sem.at[1]).wait()
-
-    @pl.when(has_up)
-    def _():
-        up_copy().start()
-
-    for c in range(2):
-        whole(pk.at[c, pl.ds(0, 31 * 16)], send_sem.at[c]).wait()
-        for i in range(4):
-            @pl.when(jnp.logical_not(jnp.equal(me, 4 * (2 * i + c) + i)))
-            def _(c=c, i=i):
-                extra_out(c, i).wait_send()
-        whole(ob.at[c, pl.ds(0, 31)], back_sem.at[c]).wait()
-
-    @pl.when(is_extra)
-    def _():
-        whole(ob.at[2, pl.ds(0, 31)], back_sem.at[2]).wait()
-
-    @pl.when(has_up)
-    def _():
-        u_copy().wait_send()
-        up_copy().wait_send()
-        down_copy().wait_recv()
-
-    @pl.when(has_down)
-    def _():
-        down_copy().wait_send()
-        u_copy().wait_recv()
-        up_copy().wait_recv()
-
-
-def update_kernel(
-    sg, above, below, ub, rd, ru,
-    sig_out, new_out,
-    km, sf, es_h, es_l, el_h, el_l,
-):
     row48 = lax.broadcasted_iota(jnp.int32, (48, 128), 0)
     lane48 = lax.broadcasted_iota(jnp.int32, (48, 128), 1)
     lane8 = lax.broadcasted_iota(jnp.int32, (8, 128), 1)
@@ -307,17 +257,6 @@
             ref[index, 0:128, 128:256] = m
             ref[index, 128:256, 0:128] = -m
             ref[index, 128:256, 128:256] = r
-
-    for array in range(4):
-        def take(t, array=array):
-            return sg[array, t] if array < 2 else (above[t] if array == 2 else below[t])
-
-        def rows(q, carry, array=array, take=take):
-            for j, r in enumerate(to_rows(take(3 * q), take(3 * q + 1), take(3 * q + 2), lane8)):
-                km[pl.ds(array * 384 + 4 * q + j, 8, stride=48), :] = r
-            return carry
-
-        lax.fori_loop(0, 12, rows, 0)
 
     def flat_store(re, im, out, blk):
         for part, x in ((0, re), (1, im)):
@@ -352,7 +291,17 @@
 
         return carry
 
-    lax.fori_loop(0, 16, unpack, 0)
+    def to_matrices(array):
+        def take(t):
+            return sg[array, t] if array < 2 else (above[t] if array == 2 else below[t])
+
+        def rows(q, carry):
+            for j, r in enumerate(to_rows(take(3 * q), take(3 * q + 1), take(3 * q + 2), lane8)):
+                km[pl.ds(array * 384 + 4 * q + j, 8, stride=48), :] = r
+            return carry
+
+        lax.fori_loop(0, 12, rows, 0)
+        lax.fori_loop(4 * array, 4 * array + 4, unpack, 0)
 
     lane96 = lax.broadcasted_iota(jnp.int32, (96, 128), 1)
 
@@ -383,10 +332,6 @@
         store_pair(el_h, el_l, 16 + blk, flip(matrix(ub, blk, 0)), flip(matrix(ub, blk, 1)))
         return carry
 
-    lax.fori_loop(0, 8, diag_prep, 0)
-    lax.fori_loop(0, 8, upper_prep, 0)
-    lax.fori_loop(0, 4, below_prep, 0)
-
     transposed = (((1,), (1,)), ((), ()))
 
     def term(left, middle):
@@ -394,16 +339,100 @@
         xh, xl = split(x)
         return dot3(xh, xl, el_h[left], el_l[left], transposed)
 
-    def combine(blk, carry):
-        c = blk // 4
-        e = blk % 4
-        low = jnp.where(c == 0, 12 + e, e)
-        high = jnp.where(c == 0, 4 + e, 8 + e)
-        total = term(blk, blk) + term(16 + blk, low) + term(8 + blk, high)
-        flat_store(total[:, :128], total[:, 128:], new_out, blk)
-        return carry
-
-    lax.fori_loop(0, 8, combine, 0)
+    def add_terms(*pairs):
+        def one(e, carry):
+            for blk, left, middle, first in pairs:
+                value = term(left + e, middle + e)
+                if first:
+                    total[blk + e] = value
+                else:
+                    total[blk + e] += value
+            return carry
+
+        lax.fori_loop(0, 4, one, 0)
+
+    def finish(c):
+        def one(blk, carry):
+            flat_store(total[blk, :, :128], total[blk, :, 128:], new_out, blk)
+            return carry
+
+        lax.fori_loop(4 * c, 4 * c + 4, one, 0)
+
+    def convolve_cell(c):
+        def step(j, inner):
+            slot = jnp.where(j == 0, c, 2)
+            tile = jnp.where(j == 0, me, PEERS + my_i)
+            convolve(slot, c, tile)
+            return inner
+
+        lax.fori_loop(0, 1 + jnp.where(jnp.logical_and(is_extra, my_c == c), 1, 0), step, 0)
+
+    load_rd.wait()
+    lax.fori_loop(0, 8, diag_prep, 0)
+    convolve_cell(0)
+    load_ru.wait()
+    lax.fori_loop(0, 8, upper_prep, 0)
+    convolve_cell(1)
+
+    @pl.when(has_down)
+    def _():
+        u_copy().wait_recv()
+
+    lax.fori_loop(0, 4, below_prep, 0)
+
+    whole(sg.at[0], sig_sem.at[0]).wait()
+
+    @pl.when(has_down)
+    def _():
+        down_copy().start()
+
+    to_matrices(0)
+    add_terms((0, 0, 0, True), (4, 20, 0, True))
+
+    @pl.when(has_up)
+    def _():
+        down_copy().wait_recv()
+
+    to_matrices(2)
+    add_terms((4, 12, 8, False))
+    whole(sg.at[1], sig_sem.at[1]).wait()
+
+    @pl.when(has_up)
+    def _():
+        up_copy().start()
+
+    to_matrices(1)
+    add_terms((4, 4, 4, False), (0, 8, 4, False))
+    finish(1)
+
+    @pl.when(has_down)
+    def _():
+        up_copy().wait_recv()
+
+    to_matrices(3)
+    add_terms((0, 16, 12, False))
+    finish(0)
+
+    for c in range(2):
+        whole(pk.at[c, pl.ds(0, 31 * 16)], send_sem.at[c]).wait()
+        for i in range(4):
+            @pl.when(jnp.logical_not(jnp.equal(me, 4 * (2 * i + c) + i)))
+            def _(c=c, i=i):
+                extra_out(c, i).wait_send()
+        whole(ob.at[c, pl.ds(0, 31)], back_sem.at[c]).wait()
+
+    @pl.when(is_extra)
+    def _():
+        whole(ob.at[2, pl.ds(0, 31)], back_sem.at[2]).wait()
+
+    @pl.when(has_up)
+    def _():
+        u_copy().wait_send()
+        up_copy().wait_send()
+
+    @pl.when(has_down)
+    def _():
+        down_copy().wait_send()
 
 
 def flat_view(x):
@@ -421,43 +450,35 @@
     vmem = pl.BlockSpec(memory_space=pltpu.VMEM)
     hbm = pl.BlockSpec(memory_space=pl.ANY)
     dma = pltpu.SemaphoreType.DMA
-    sg, above, below, ub = pl.pallas_call(
-        exchange_kernel,
-        out_shape=[
-            jax.ShapeDtypeStruct((2, HALF, 8, 128), F32),
-            jax.ShapeDtypeStruct((HALF, 8, 128), F32),
-            jax.ShapeDtypeStruct((HALF, 8, 128), F32),
-            jax.ShapeDtypeStruct((4, 144, 128), F32),
-        ],
-        in_specs=[hbm] * 3 + [vmem] * 4,
-        out_specs=[vmem] * 4,
+    sigma, new = pl.pallas_call(
+        kernel,
+        out_shape=[jax.ShapeDtypeStruct((8, 144, 128), F32)] * 2,
+        in_specs=[hbm] * 4 + [vmem] * 4,
+        out_specs=[vmem] * 2,
         scratch_shapes=[
             pltpu.VMEM((8, 160, 128), F32),
             pltpu.VMEM((8, 160, 128), F32),
             pltpu.VMEM((2, 640, 128), F32),
             pltpu.VMEM((3, PEERS, 16, 128), F32),
             pltpu.VMEM((3, PEERS, 8, 128), F32),
-            dma((2, 2)), dma((2,)), dma((2,)), dma((2, 4)), dma((3,)), dma((3,)), dma((2,)), dma((2,)), dma((3,)), dma((3,)),
-        ],
-        compiler_params=pltpu.CompilerParams(collective_id=0, has_side_effects=True, vmem_limit_bytes=VMEM_LIMIT),
-        name="exchange",
-    )(g, w, ru, *constants)
-    sigma, new = pl.pallas_call(
-        update_kernel,
-        out_shape=[jax.ShapeDtypeStruct((8, 144, 128), F32)] * 2,
-        in_specs=[vmem] * 6,
-        out_specs=[vmem] * 2,
-        scratch_shapes=[
+            pltpu.VMEM((2, HALF, 8, 128), F32),
+            pltpu.VMEM((HALF, 8, 128), F32),
+            pltpu.VMEM((HALF, 8, 128), F32),
+            pltpu.VMEM((4, 144, 128), F32),
+            pltpu.VMEM((8, 144, 128), F32),
+            pltpu.VMEM((8, 144, 128), F32),
             pltpu.VMEM((4 * 384, 128), F32),
             pltpu.VMEM((2, 96, 128), F32),
             pltpu.VMEM((16, 256, 256), BF16),
             pltpu.VMEM((16, 256, 256), BF16),
             pltpu.VMEM((24, 256, 256), BF16),
             pltpu.VMEM((24, 256, 256), BF16),
+            pltpu.VMEM((8, 96, 256), F32),
+            dma((2, 2)), dma((2,)), dma((2,)), dma((2, 4)), dma((3,)), dma((3,)), dma((2,)), dma((3,)), dma((3,)),
         ],
-        compiler_params=pltpu.CompilerParams(vmem_limit_bytes=VMEM_LIMIT),
+        compiler_params=pltpu.CompilerParams(collective_id=0, has_side_effects=True, vmem_limit_bytes=VMEM_LIMIT),
         name="update",
-    )(sg, above, below, ub, rd, ru)
+    )(g, w, rd, ru, *constants)
     return from_flat(sigma), from_flat(new)
 
 

time: 64.1 us -> 54.3 us (0.85)
  Pallas kernels: 63.2 us -> 50.5 us
  local copies, waits for them, and re-layouts: 0 us -> 2.8 us
    pallas_call x2 -> x1, Pallas kernels: 63.2 us -> 50.5 us  [shards(): pl.pallas_call(kernel, out_shape=[jax.ShapeDtypeStruct((8, 144, 128), F32...]
    unnamed x0 -> x4, local copies, waits for them, and re-layouts: none -> 2.8 us
where the time goes in v1:
time: 54.3 us; the launch traced here: 53.9 us
  Pallas kernels  50.5 us (93%)
  local copies, waits for them, and re-layouts  2.8 us (5%)
  between operations  0.65 us (1%)
    pallas_call x1, Pallas kernels, shards(): pl.pallas_call(kernel, out_shape=[jax.ShapeDtypeStruct((8, 144, 128), F32...  50.5 us
    unnamed x4, local copies, waits for them, and re-layouts  2.8 us

profile of v1, /device:TPU:4, one launch (start us, length us, event | category | flops | bytes accessed | tf_op | source)
XLA Modules:
  0.0 53.9 jit_solution(10083378193591648619)
XLA Ops:
  0.6 50.5 %update.1 = (f32[8,144,128]{2,1,0:T(8,128)}, f32[8,144,128]{2,1,0:T(8,128)}) custom-call(f32[8,144,128]{2,1,0:T(8,128)} %bitcast.32, f32[8,144,128]{2,1,0:T(8,128)} %bitcast.33, f32[8,144,128]{2,1,0:T(8,128)} %bitcast.34, f32[8,144,128]{2,1,0:T(8,128)} %bitcast.35, bf16[512,256]{1,0:T(8,128)(2,1)} %constant.8.clone.fh, bf16[512,256]{1,0:T(8,128)(2,1)} %constant.9.clone.fl, ...), custom_call_target="tpu_custom_call" | custom-call | tf_op jit(solution)/shard_map/update/pallas_call | solution.py:453
  51.1 0.0 copy-start
  51.2 2.0 %copy.18 = f32[2,4,2,9216]{3,2,1,0:T(2,128)} copy(f32[2,4,2,9216]{3,2,1,0:T(2,128)} %bitcast.31) | data formatting | bytes 1179648
  53.1 0.0 copy-done
  53.1 0.8 %copy.19 = f32[2,4,2,9216]{3,2,1,0:T(2,128)} copy(f32[2,4,2,9216]{3,2,1,0:T(2,128)S(1)} %bitcast.30) | data formatting | bytes 1179648
Async XLA Ops:
  51.1 2.0 %copy-start = (f32[8,144,128]{2,1,0:T(8,128)S(1)}, f32[8,144,128]{2,1,0:T(8,128)}, u32[]{:S(2)}) copy-start(f32[8,144,128]{2,1,0:T(8,128)} %get-tuple-element.5) | copy-start | bytes 1769476

commit v2 on v1

--- a/solution.py
+++ b/solution.py
@@ -16,6 +16,7 @@
 HALF = 36
 F32 = jnp.float32
 BF16 = jnp.bfloat16
+PIECES = 4
 VMEM_LIMIT = 56 * 1024 * 1024
 
 
@@ -258,20 +259,16 @@
             ref[index, 128:256, 0:128] = -m
             ref[index, 128:256, 128:256] = r
 
-    def flat_store(re, im, out, blk):
-        for part, x in ((0, re), (1, im)):
-            sf[part] = x
+    def flat_store(matrices, out, blk):
         for part in range(2):
-            tiles = to_tiles(*(sf[part, pl.ds(j, 24, stride=4), :] for j in range(4)), lane24)
+            tiles = to_tiles(*(matrices[blk, part, pl.ds(j, 24, stride=4), :] for j in range(4)), lane24)
             for j in range(3):
                 out[blk, pl.ds(2 * j + part, 24, stride=6), :] = tiles[j]
 
-    def unpack(index, carry):
-        array = index // 4
-        e = index % 4
-        base = array * 384 + 2 * e * 48
-        kr = km[pl.ds(pl.multiple_of(base, 8), 48), :]
-        ki = km[pl.ds(pl.multiple_of(base + 48, 8), 48), :]
+    def unpack(index):
+        base = 96 * index
+        kr = km[base:base + 48, :]
+        ki = km[base + 48:base + 96, :]
         krt = -jnp.concatenate([kr, zero48], 0).T
         kit = jnp.concatenate([ki, zero48], 0).T
         less, same = lane48 < row48, lane48 == row48
@@ -284,32 +281,27 @@
         re = jnp.concatenate([jnp.where(inside48, top_r, 0.0), jnp.where(inside48, low_r, 0.0)], 0)
         im = jnp.concatenate([jnp.where(inside48, top_i, 0.0), jnp.where(inside48, low_i, 0.0)], 0)
         store_pair(es_h, es_l, index, re, im)
-
-        @pl.when(index < 8)
-        def _():
-            flat_store(re, im, sig_out, index)
-
-        return carry
+        if index < 8:
+            sf[index, 0] = re
+            sf[index, 1] = im
 
     def to_matrices(array):
         def take(t):
             return sg[array, t] if array < 2 else (above[t] if array == 2 else below[t])
 
-        def rows(q, carry):
+        for q in range(12):
             for j, r in enumerate(to_rows(take(3 * q), take(3 * q + 1), take(3 * q + 2), lane8)):
                 km[pl.ds(array * 384 + 4 * q + j, 8, stride=48), :] = r
-            return carry
-
-        lax.fori_loop(0, 12, rows, 0)
-        lax.fori_loop(4 * array, 4 * array + 4, unpack, 0)
+        for index in range(4 * array, 4 * array + 4):
+            unpack(index)
 
     lane96 = lax.broadcasted_iota(jnp.int32, (96, 128), 1)
 
     def matrix(source, blk, part):
         u = [source[blk, pl.ds(2 * j + part, 24, stride=6), :] for j in range(3)]
         for j, r in enumerate(to_rows(*u, lane24)):
-            sf[part, pl.ds(j, 24, stride=4), :] = r
-        return jnp.where(lane96 < B, sf[part], 0.0)
+            sf[blk, part, pl.ds(j, 24, stride=4), :] = r
+        return jnp.where(lane96 < B, sf[blk, part], 0.0)
 
     def flip(x):
         return jnp.concatenate([x, zero32], 0).T[:96]
@@ -334,29 +326,28 @@
 
     transposed = (((1,), (1,)), ((), ()))
 
-    def term(left, middle):
-        x = dot3(el_h[left, 0:96, :], el_l[left, 0:96, :], es_h[middle], es_l[middle])
-        xh, xl = split(x)
-        return dot3(xh, xl, el_h[left], el_l[left], transposed)
-
-    def add_terms(*pairs):
-        def one(e, carry):
-            for blk, left, middle, first in pairs:
-                value = term(left + e, middle + e)
-                if first:
-                    total[blk + e] = value
-                else:
-                    total[blk + e] += value
-            return carry
-
-        lax.fori_loop(0, 4, one, 0)
+    def add_terms(middle, pairs):
+        for e in range(4):
+            left_h = jnp.concatenate([el_h[left + e, 0:96, :] for _, left, _ in pairs], 0)
+            left_l = jnp.concatenate([el_l[left + e, 0:96, :] for _, left, _ in pairs], 0)
+            xh, xl = split(dot3(left_h, left_l, es_h[middle + e], es_l[middle + e]))
+            for i, (blk, left, first) in enumerate(pairs):
+                rows = slice(96 * i, 96 * i + 96)
+                value = dot3(xh[rows], xl[rows], el_h[left + e], el_l[left + e], transposed)
+                for part in range(2):
+                    half = value[:, 128 * part:128 * part + 128]
+                    if first:
+                        total[blk + e, part] = half
+                    else:
+                        total[blk + e, part] += half
 
     def finish(c):
-        def one(blk, carry):
-            flat_store(total[blk, :, :128], total[blk, :, 128:], new_out, blk)
-            return carry
-
-        lax.fori_loop(4 * c, 4 * c + 4, one, 0)
+        for blk in range(4 * c, 4 * c + 4):
+            flat_store(total, new_out, blk)
+
+    def sigma_flat():
+        for blk in range(8):
+            flat_store(sf, sig_out, blk)
 
     def convolve_cell(c):
         def step(j, inner):
@@ -387,30 +378,31 @@
         down_copy().start()
 
     to_matrices(0)
-    add_terms((0, 0, 0, True), (4, 20, 0, True))
+    add_terms(0, ((0, 0, True), (4, 20, True)))
+    whole(sg.at[1], sig_sem.at[1]).wait()
 
     @pl.when(has_up)
     def _():
+        up_copy().start()
+
+    to_matrices(1)
+    add_terms(4, ((4, 4, False), (0, 8, False)))
+
+    @pl.when(has_up)
+    def _():
         down_copy().wait_recv()
 
     to_matrices(2)
-    add_terms((4, 12, 8, False))
-    whole(sg.at[1], sig_sem.at[1]).wait()
-
-    @pl.when(has_up)
-    def _():
-        up_copy().start()
-
-    to_matrices(1)
-    add_terms((4, 4, 4, False), (0, 8, 4, False))
+    add_terms(8, ((4, 12, False),))
     finish(1)
+    sigma_flat()
 
     @pl.when(has_down)
     def _():
         up_copy().wait_recv()
 
     to_matrices(3)
-    add_terms((0, 16, 12, False))
+    add_terms(12, ((0, 16, False),))
     finish(0)
 
     for c in range(2):
@@ -433,6 +425,18 @@
     @pl.when(has_down)
     def _():
         down_copy().wait_send()
+
+
+def publish_kernel(a, b, a_out, b_out, sems):
+    copies = []
+    for i, (src, dst) in enumerate(((a, a_out), (b, b_out))):
+        for j in range(PIECES):
+            part = pl.ds(j * (8 // PIECES), 8 // PIECES)
+            copies.append(pltpu.make_async_copy(src.at[part], dst.at[part], sems.at[i, j]))
+    for copy in copies:
+        copy.start()
+    for copy in copies:
+        copy.wait()
 
 
 def flat_view(x):
@@ -452,7 +456,7 @@
     dma = pltpu.SemaphoreType.DMA
     sigma, new = pl.pallas_call(
         kernel,
-        out_shape=[jax.ShapeDtypeStruct((8, 144, 128), F32)] * 2,
+        out_shape=[pltpu.VMEM((8, 144, 128), F32)] * 2,
         in_specs=[hbm] * 4 + [vmem] * 4,
         out_specs=[vmem] * 2,
         scratch_shapes=[
@@ -468,17 +472,25 @@
             pltpu.VMEM((8, 144, 128), F32),
             pltpu.VMEM((8, 144, 128), F32),
             pltpu.VMEM((4 * 384, 128), F32),
-            pltpu.VMEM((2, 96, 128), F32),
+            pltpu.VMEM((8, 2, 96, 128), F32),
             pltpu.VMEM((16, 256, 256), BF16),
             pltpu.VMEM((16, 256, 256), BF16),
             pltpu.VMEM((24, 256, 256), BF16),
             pltpu.VMEM((24, 256, 256), BF16),
-            pltpu.VMEM((8, 96, 256), F32),
+            pltpu.VMEM((8, 2, 96, 128), F32),
             dma((2, 2)), dma((2,)), dma((2,)), dma((2, 4)), dma((3,)), dma((3,)), dma((2,)), dma((3,)), dma((3,)),
         ],
         compiler_params=pltpu.CompilerParams(collective_id=0, has_side_effects=True, vmem_limit_bytes=VMEM_LIMIT),
         name="update",
     )(g, w, rd, ru, *constants)
+    sigma, new = pl.pallas_call(
+        publish_kernel,
+        out_shape=[jax.ShapeDtypeStruct((8, 144, 128), F32)] * 2,
+        in_specs=[vmem] * 2,
+        out_specs=[hbm] * 2,
+        scratch_shapes=[dma((2, PIECES))],
+        name="publish",
+    )(*(pltpu.with_memory_space_constraint(x, pltpu.VMEM) for x in (sigma, new)))
     return from_flat(sigma), from_flat(new)
 
 

time: 54.3 us -> 45.7 us (0.84)
  Pallas kernels: 50.5 us -> 45 us
  local copies, waits for them, and re-layouts: 2.8 us -> 0 us
    pallas_call x1 -> x2, Pallas kernels: 50.5 us -> 45 us  [the longest x1 43.9 us: shards(): pl.pallas_call(kernel, out_shape=[pltpu.VMEM((8, 144, 128), F32)] * 2, in...]
    unnamed x4 -> x0, local copies, waits for them, and re-layouts: 2.8 us -> none
where the time goes in v2:
time: 45.7 us; the launch traced here: 45.6 us
  Pallas kernels  45 us (98%)
  between operations  0.64 us (1%)
    pallas_call x1, Pallas kernels, shards(): pl.pallas_call(kernel, out_shape=[pltpu.VMEM((8, 144, 128), F32)] * 2, in...  43.9 us
    pallas_call x1, Pallas kernels, shards(): pl.pallas_call(publish_kernel, out_shape=[jax.ShapeDtypeStruct((8, 144, 1...  1.07 us

profile of v2, /device:TPU:4, one launch (start us, length us, event | category | flops | bytes accessed | tf_op | source)
XLA Modules:
  0.0 45.6 jit_solution(1119758916638198772)
XLA Ops:
  0.6 43.9 %update.1 = (f32[8,144,128]{2,1,0:T(8,128)S(1)}, f32[8,144,128]{2,1,0:T(8,128)S(1)}) custom-call(f32[8,144,128]{2,1,0:T(8,128)} %bitcast.30, f32[8,144,128]{2,1,0:T(8,128)} %bitcast.31, f32[8,144,128]{2,1,0:T(8,128)} %bitcast.32, f32[8,144,128]{2,1,0:T(8,128)} %bitcast.33, bf16[512,256]{1,0:T(8,128)(2,1)} %constant.8.clone.fh, ...), custom_call_target="tpu_custom_call" | custom-call | tf_op jit(solution)/shard_map/update/pallas_call | solution.py:457
  44.5 1.1 %publish.1 = (f32[8,144,128]{2,1,0:T(8,128)}, f32[8,144,128]{2,1,0:T(8,128)}) custom-call(f32[8,144,128]{2,1,0:T(8,128)S(1)} %get-tuple-element.6.a, f32[8,144,128]{2,1,0:T(8,128)S(1)} %get-tuple-element.7.b), custom_call_target="tpu_custom_call" | custom-call | tf_op jit(solution)/shard_map/publish/pallas_call | solution.py:486

commit v3 on v2

--- a/solution.py
+++ b/solution.py
@@ -55,10 +55,10 @@
 
 
 def kernel(
-    g_hbm, w_hbm, rd_hbm, u_hbm, fh, fl, ih, il,
+    g_hbm, w_hbm, rd_hbm, u_hbm, fh_hbm, fl_hbm, ih_hbm, il_hbm,
     sig_out, new_out,
-    gv, wv, pk, rv, ob, sg, above, below, ub, rd, ru, km, sf, es_h, es_l, el_h, el_l, total,
-    load_sem, ret_sem, send_sem, xsend_sem, recv_sem, back_sem, sig_sem, hop_send, hop_recv,
+    fh, fl, ih, il, gv, wv, pk, rv, ob, sg, above, below, ub, rd, ru, km, sf, es_h, es_l, el_h, el_l, total,
+    load_sem, ret_sem, mat_sem, send_sem, xsend_sem, recv_sem, back_sem, sig_sem, hop_send, hop_recv,
 ):
     me = lax.axis_index("energy")
     k = lax.axis_index("cell")
@@ -69,14 +69,11 @@
     has_up = k < 7
     has_down = k > 0
 
-    for c in range(2):
-        pltpu.make_async_copy(g_hbm.at[pl.ds(4 * c, 4)], gv.at[pl.ds(4 * c, 4), pl.ds(0, 144)], load_sem.at[c, 0]).start()
-        pltpu.make_async_copy(w_hbm.at[pl.ds(4 * c, 4)], wv.at[pl.ds(4 * c, 4), pl.ds(0, 144)], load_sem.at[c, 1]).start()
-
-    load_rd = pltpu.make_async_copy(rd_hbm, rd, ret_sem.at[0])
-    load_ru = pltpu.make_async_copy(u_hbm, ru, ret_sem.at[1])
-    load_rd.start()
-    load_ru.start()
+    def load_cell(c):
+        for j, (source, target) in enumerate(((g_hbm, gv), (w_hbm, wv))):
+            pltpu.make_async_copy(source.at[pl.ds(4 * c, 4)], target.at[pl.ds(4 * c, 4), pl.ds(0, 144)], load_sem.at[c, j]).start()
+
+    load_cell(0)
 
     barrier = pltpu.get_barrier_semaphore()
 
@@ -93,6 +90,16 @@
     @pl.when(has_down)
     def _():
         pl.semaphore_signal(barrier, inc=1, device_id={"cell": k - 1}, device_id_type=MESH)
+
+    load_cell(1)
+    load_rd = pltpu.make_async_copy(rd_hbm, rd, ret_sem.at[0])
+    load_ru = pltpu.make_async_copy(u_hbm, ru, ret_sem.at[1])
+    load_mats = [
+        pltpu.make_async_copy(source, target, mat_sem.at[i])
+        for i, (source, target) in enumerate(((fh_hbm, fh), (fl_hbm, fl), (ih_hbm, ih), (il_hbm, il)))
+    ]
+    for copy in (*load_mats, load_rd, load_ru):
+        copy.start()
 
     row = lax.broadcasted_iota(jnp.int32, (40, 128), 0)
     lane = lax.broadcasted_iota(jnp.int32, (40, 128), 1)
@@ -109,7 +116,7 @@
                 (g_hbm, w_hbm)[which].at[pl.ds(4 * c, 4)], source.at[pl.ds(4 * c, 4), pl.ds(0, 144)], load_sem.at[c, which]
             ).wait()
 
-            def one(e, carry):
+            for e in range(4):
                 blk = 4 * c + e
                 first, far = [], []
                 for part in range(2):
@@ -123,9 +130,6 @@
                 base = which * 8 + 2 * e
                 pk[c, pl.ds(base, 40, stride=16), :] = re
                 pk[c, pl.ds(base + 1, 40, stride=16), :] = im
-                return carry
-
-            lax.fori_loop(0, 4, one, 0)
 
     def outgoing(c, p):
         return pltpu.make_async_remote_copy(
@@ -141,11 +145,17 @@
 
     def send(c):
         def start(i, carry):
-            outgoing(c, lax.rem(me + i, PEERS)).start()
+            p = 2 * lax.rem(me // 2 + 16 + jnp.where(i % 2 == 1, (i % 16 + 1) // 2, -((i % 16) // 2)), 16) + i // 16
+
+            @pl.when(p != me)
+            def _():
+                outgoing(c, p).start()
+
             return carry
 
         pltpu.make_async_copy(pk.at[c, pl.ds(me * 16, 16)], rv.at[c, me], recv_sem.at[c]).start()
-        lax.fori_loop(1, PEERS, start, 0)
+        lax.fori_loop(0, PEERS, start, 0)
+
         for i in range(4):
             mine = jnp.equal(me, 4 * (2 * i + c) + i)
 
@@ -156,6 +166,7 @@
             @pl.when(mine)
             def _(i=i):
                 pltpu.make_async_copy(pk.at[c, pl.ds((PEERS + i) * 16, 16)], rv.at[2, me], recv_sem.at[2]).start()
+
 
     pack(0)
     pl.semaphore_wait(barrier, 31 + has_up.astype(jnp.int32) + has_down.astype(jnp.int32))
@@ -175,6 +186,20 @@
             device_id={"cell": k - 1}, device_id_type=MESH,
         )
 
+    def down_part(half):
+        part = pl.ds(18 * half, 18)
+        return pltpu.make_async_remote_copy(
+            src_ref=sg.at[0, part], dst_ref=above.at[part], send_sem=hop_send.at[1], recv_sem=hop_recv.at[1],
+            device_id={"cell": k - 1}, device_id_type=MESH,
+        )
+
+    def up_part(half):
+        part = pl.ds(18 * half, 18)
+        return pltpu.make_async_remote_copy(
+            src_ref=sg.at[1, part], dst_ref=below.at[part], send_sem=hop_send.at[2], recv_sem=hop_recv.at[2],
+            device_id={"cell": k + 1}, device_id_type=MESH,
+        )
+
     def up_copy():
         return pltpu.make_async_remote_copy(
             src_ref=sg.at[1], dst_ref=below, send_sem=hop_send.at[2], recv_sem=hop_recv.at[2],
@@ -194,9 +219,12 @@
         below[...] = jnp.zeros_like(below)
         ub[...] = jnp.zeros_like(ub)
 
+    def place(tile):
+        return (tile % 2) * 18 + tile // 2
+
     def back(slot, c, tile, p):
         return pltpu.make_async_remote_copy(
-            src_ref=ob.at[slot, p], dst_ref=sg.at[c, tile], send_sem=back_sem.at[slot], recv_sem=sig_sem.at[c],
+            src_ref=ob.at[slot, p], dst_ref=sg.at[c, place(tile)], send_sem=back_sem.at[slot], recv_sem=sig_sem.at[c, tile % 2],
             device_id={"energy": p}, device_id_type=MESH,
         )
 
@@ -223,7 +251,7 @@
         on_diagonal = position == ((position * 43241) >> 22) * 97
         ob[slot] = jnp.where(on_diagonal, out[:, 128:], out[:, :128]).reshape(PEERS, 8, 128)
 
-        pltpu.make_async_copy(ob.at[slot, me], sg.at[c, tile], sig_sem.at[c]).start()
+        pltpu.make_async_copy(ob.at[slot, me], sg.at[c, place(tile)], sig_sem.at[c, tile % 2]).start()
 
         def start(i, carry):
             back(slot, c, tile, lax.rem(me + i, PEERS)).start()
@@ -287,6 +315,7 @@
 
     def to_matrices(array):
         def take(t):
+            t = place(t)
             return sg[array, t] if array < 2 else (above[t] if array == 2 else below[t])
 
         for q in range(12):
@@ -360,6 +389,8 @@
 
     load_rd.wait()
     lax.fori_loop(0, 8, diag_prep, 0)
+    for copy in load_mats:
+        copy.wait()
     convolve_cell(0)
     load_ru.wait()
     lax.fori_loop(0, 8, upper_prep, 0)
@@ -371,19 +402,21 @@
 
     lax.fori_loop(0, 4, below_prep, 0)
 
-    whole(sg.at[0], sig_sem.at[0]).wait()
-
-    @pl.when(has_down)
-    def _():
-        down_copy().start()
+    for half in range(2):
+        whole(sg.at[0, pl.ds(18 * half, 18)], sig_sem.at[0, half]).wait()
+
+        @pl.when(has_down)
+        def _(half=half):
+            down_part(half).start()
 
     to_matrices(0)
     add_terms(0, ((0, 0, True), (4, 20, True)))
-    whole(sg.at[1], sig_sem.at[1]).wait()
-
-    @pl.when(has_up)
-    def _():
-        up_copy().start()
+    for half in range(2):
+        whole(sg.at[1, pl.ds(18 * half, 18)], sig_sem.at[1, half]).wait()
+
+        @pl.when(has_up)
+        def _(half=half):
+            up_part(half).start()
 
     to_matrices(1)
     add_terms(4, ((4, 4, False), (0, 8, False)))
@@ -457,9 +490,13 @@
     sigma, new = pl.pallas_call(
         kernel,
         out_shape=[pltpu.VMEM((8, 144, 128), F32)] * 2,
-        in_specs=[hbm] * 4 + [vmem] * 4,
+        in_specs=[hbm] * 8,
         out_specs=[vmem] * 2,
         scratch_shapes=[
+            pltpu.VMEM((512, 256), BF16),
+            pltpu.VMEM((512, 256), BF16),
+            pltpu.VMEM((256, 512), BF16),
+            pltpu.VMEM((256, 512), BF16),
             pltpu.VMEM((8, 160, 128), F32),
             pltpu.VMEM((8, 160, 128), F32),
             pltpu.VMEM((2, 640, 128), F32),
@@ -478,7 +515,7 @@
             pltpu.VMEM((24, 256, 256), BF16),
             pltpu.VMEM((24, 256, 256), BF16),
             pltpu.VMEM((8, 2, 96, 128), F32),
-            dma((2, 2)), dma((2,)), dma((2,)), dma((2, 4)), dma((3,)), dma((3,)), dma((2,)), dma((3,)), dma((3,)),
+            dma((2, 2)), dma((2,)), dma((4,)), dma((2,)), dma((2, 4)), dma((3,)), dma((3,)), dma((2, 2)), dma((3,)), dma((3,)),
         ],
         compiler_params=pltpu.CompilerParams(collective_id=0, has_side_effects=True, vmem_limit_bytes=VMEM_LIMIT),
         name="update",

time: 45.7 us -> 43.3 us (0.947)
  Pallas kernels: 45 us -> 42.6 us
    pallas_call x1, Pallas kernels: 43.9 us -> 41.5 us  [shards(): pl.pallas_call(kernel, out_shape=[pltpu.VMEM((8, 144, 128), F32)] * 2, in...]
where the time goes in v3:
time: 43.3 us; the launch traced here: 43.2 us
  Pallas kernels  42.6 us (98%)
  between operations  0.64 us (1%)
    pallas_call x1, Pallas kernels, shards(): pl.pallas_call(kernel, out_shape=[pltpu.VMEM((8, 144, 128), F32)] * 2, in...  41.5 us
    pallas_call x1, Pallas kernels, shards(): pl.pallas_call(publish_kernel, out_shape=[jax.ShapeDtypeStruct((8, 144, 1...  1.07 us

profile of v3, /device:TPU:4, one launch (start us, length us, event | category | flops | bytes accessed | tf_op | source)
XLA Modules:
  0.0 43.2 jit_solution(17095618473922564758)
XLA Ops:
  0.6 41.5 %update.1 = (f32[8,144,128]{2,1,0:T(8,128)S(1)}, f32[8,144,128]{2,1,0:T(8,128)S(1)}) custom-call(f32[8,144,128]{2,1,0:T(8,128)} %bitcast.30, f32[8,144,128]{2,1,0:T(8,128)} %bitcast.31, f32[8,144,128]{2,1,0:T(8,128)} %bitcast.32, f32[8,144,128]{2,1,0:T(8,128)} %bitcast.33, bf16[512,256]{1,0:T(8,128)(2,1)} %constant.8.clone.fh_hbm, ...), custom_call_target="tpu_custom_call" | custom-call | tf_op jit(solution)/shard_map/update/pallas_call | solution.py:490
  42.2 1.1 %publish.1 = (f32[8,144,128]{2,1,0:T(8,128)}, f32[8,144,128]{2,1,0:T(8,128)}) custom-call(f32[8,144,128]{2,1,0:T(8,128)S(1)} %get-tuple-element.6.a, f32[8,144,128]{2,1,0:T(8,128)S(1)} %get-tuple-element.7.b), custom_call_target="tpu_custom_call" | custom-call | tf_op jit(solution)/shard_map/publish/pallas_call | solution.py:523

commit v4 on v3

--- a/solution.py
+++ b/solution.py
@@ -30,14 +30,12 @@
     k = np.arange(NE)
     angle = 2.0 * np.pi / (4 * NE) * ((n[None, :] * (1 - 4 * k[:, None])) % (4 * NE))
     forward = np.zeros((2, 2, NE, NE, 2))
-    inverse = np.zeros((NE, 2, 2, 2, NE))
     scale = NE ** -0.5 / NE
     for part in range(2):
         forward[part, 0, :, :, part] = np.cos(angle)
         forward[part, 1, :, :, part] = np.sin(angle)
-        inverse[:, part, part, 0, :] = np.cos(angle).T * scale
-        inverse[:, part, part, 1, :] = np.sin(angle).T * scale
-    return forward.reshape(512, 256), inverse.reshape(256, 512)
+    inverse = np.concatenate([np.cos(angle).T, np.sin(angle).T], 1) * scale
+    return forward.reshape(512, 256), inverse
 
 
 def split(x):
@@ -224,7 +222,7 @@
 
     def back(slot, c, tile, p):
         return pltpu.make_async_remote_copy(
-            src_ref=ob.at[slot, p], dst_ref=sg.at[c, place(tile)], send_sem=back_sem.at[slot], recv_sem=sig_sem.at[c, tile % 2],
+            src_ref=ob.at[slot, pl.ds(p * 8, 8)], dst_ref=sg.at[c, place(tile)], send_sem=back_sem.at[slot], recv_sem=sig_sem.at[c, tile % 2],
             device_id={"energy": p}, device_id_type=MESH,
         )
 
@@ -243,18 +241,19 @@
         yy_i = yrg * yiw + yig * yrw
         xy_r = (xrg * yrw - xig * yiw) + (yrg * xrw - yig * xiw)
         xy_i = (xrg * yiw + xig * yrw) + (yrg * xiw + yig * xrw)
-        main = jnp.concatenate([-xy_r, -xy_i, xx_r - yy_r, xx_i - yy_i], 0)
-        diag = jnp.concatenate([-xx_r, -xx_i, -yy_r, -yy_i], 0)
-        zh, zl = split(jnp.concatenate([main, diag], 1))
+        products = jnp.concatenate([jnp.concatenate(z, 0) for z in ((xx_r, xx_i), (yy_r, yy_i), (xy_r, xy_i))], 1)
+        zh, zl = split(products)
         out = dot3(ih[...], il[...], zh, zl)
-        position = tile * 128 + lax.broadcasted_iota(jnp.int32, (256, 128), 1)
+        xx, yy, xy = (out[:, 128 * j:128 * j + 128] for j in range(3))
+        position = tile * 128 + lax.broadcasted_iota(jnp.int32, (128, 128), 1)
         on_diagonal = position == ((position * 43241) >> 22) * 97
-        ob[slot] = jnp.where(on_diagonal, out[:, 128:], out[:, :128]).reshape(PEERS, 8, 128)
-
-        pltpu.make_async_copy(ob.at[slot, me], sg.at[c, place(tile)], sig_sem.at[c, tile % 2]).start()
+        ob[slot, pl.ds(0, 128, stride=2), :] = -jnp.where(on_diagonal, xx, xy)
+        ob[slot, pl.ds(1, 128, stride=2), :] = jnp.where(on_diagonal, 0.0, xx) - yy
+
+        pltpu.make_async_copy(ob.at[slot, pl.ds(me * 8, 8)], sg.at[c, place(tile)], sig_sem.at[c, tile % 2]).start()
 
         def start(i, carry):
-            back(slot, c, tile, lax.rem(me + i, PEERS)).start()
+            back(slot, c, tile, lax.rem(me + PEERS + jnp.where(i % 2 == 1, 16 - i // 2, i // 2 - 16), PEERS)).start()
             return carry
 
         lax.fori_loop(1, PEERS, start, 0)
@@ -430,34 +429,37 @@
     finish(1)
     sigma_flat()
 
-    @pl.when(has_down)
-    def _():
-        up_copy().wait_recv()
-
-    to_matrices(3)
-    add_terms(12, ((0, 16, False),))
-    finish(0)
-
     for c in range(2):
         whole(pk.at[c, pl.ds(0, 31 * 16)], send_sem.at[c]).wait()
         for i in range(4):
             @pl.when(jnp.logical_not(jnp.equal(me, 4 * (2 * i + c) + i)))
             def _(c=c, i=i):
                 extra_out(c, i).wait_send()
-        whole(ob.at[c, pl.ds(0, 31)], back_sem.at[c]).wait()
+        whole(ob.at[c, pl.ds(0, 31 * 8)], back_sem.at[c]).wait()
 
     @pl.when(is_extra)
     def _():
-        whole(ob.at[2, pl.ds(0, 31)], back_sem.at[2]).wait()
+        whole(ob.at[2, pl.ds(0, 31 * 8)], back_sem.at[2]).wait()
 
     @pl.when(has_up)
     def _():
         u_copy().wait_send()
+
+    @pl.when(has_down)
+    def _():
+        down_copy().wait_send()
+
+    @pl.when(has_down)
+    def _():
+        up_copy().wait_recv()
+
+    to_matrices(3)
+    add_terms(12, ((0, 16, False),))
+    finish(0)
+
+    @pl.when(has_up)
+    def _():
         up_copy().wait_send()
-
-    @pl.when(has_down)
-    def _():
-        down_copy().wait_send()
 
 
 def publish_kernel(a, b, a_out, b_out, sems):
@@ -495,13 +497,13 @@
         scratch_shapes=[
             pltpu.VMEM((512, 256), BF16),
             pltpu.VMEM((512, 256), BF16),
-            pltpu.VMEM((256, 512), BF16),
-            pltpu.VMEM((256, 512), BF16),
+            pltpu.VMEM((128, 256), BF16),
+            pltpu.VMEM((128, 256), BF16),
             pltpu.VMEM((8, 160, 128), F32),
             pltpu.VMEM((8, 160, 128), F32),
             pltpu.VMEM((2, 640, 128), F32),
             pltpu.VMEM((3, PEERS, 16, 128), F32),
-            pltpu.VMEM((3, PEERS, 8, 128), F32),
+            pltpu.VMEM((3, PEERS * 8, 128), F32),
             pltpu.VMEM((2, HALF, 8, 128), F32),
             pltpu.VMEM((HALF, 8, 128), F32),
             pltpu.VMEM((HALF, 8, 128), F32),

time: 43.3 us -> 42.7 us (0.986)
  Pallas kernels: 42.6 us -> 41.7 us
    pallas_call x1, Pallas kernels: 41.5 us -> 40.6 us  [shards(): pl.pallas_call(kernel, out_shape=[pltpu.VMEM((8, 144, 128), F32)] * 2, in...]
where the time goes in v4:
time: 42.7 us; the launch traced here: 42.3 us
  Pallas kernels  41.7 us (98%)
  between operations  0.64 us (1%)
    pallas_call x1, Pallas kernels, shards(): pl.pallas_call(kernel, out_shape=[pltpu.VMEM((8, 144, 128), F32)] * 2, in...  40.6 us
    pallas_call x1, Pallas kernels, shards(): pl.pallas_call(publish_kernel, out_shape=[jax.ShapeDtypeStruct((8, 144, 1...  1.07 us

profile of v4, /device:TPU:4, one launch (start us, length us, event | category | flops | bytes accessed | tf_op | source)
XLA Modules:
  0.0 42.3 jit_solution(8118085763215209395)
XLA Ops:
  0.6 40.6 %update.1 = (f32[8,144,128]{2,1,0:T(8,128)S(1)}, f32[8,144,128]{2,1,0:T(8,128)S(1)}) custom-call(f32[8,144,128]{2,1,0:T(8,128)} %bitcast.30, f32[8,144,128]{2,1,0:T(8,128)} %bitcast.31, f32[8,144,128]{2,1,0:T(8,128)} %bitcast.32, f32[8,144,128]{2,1,0:T(8,128)} %bitcast.33, bf16[512,256]{1,0:T(8,128)(2,1)} %constant.8.clone.fh_hbm, ...), custom_call_target="tpu_custom_call" | custom-call | tf_op jit(solution)/shard_map/update/pallas_call | solution.py:492
  41.2 1.1 %publish.1 = (f32[8,144,128]{2,1,0:T(8,128)}, f32[8,144,128]{2,1,0:T(8,128)}) custom-call(f32[8,144,128]{2,1,0:T(8,128)S(1)} %get-tuple-element.6.a, f32[8,144,128]{2,1,0:T(8,128)S(1)} %get-tuple-element.7.b), custom_call_target="tpu_custom_call" | custom-call | tf_op jit(solution)/shard_map/publish/pallas_call | solution.py:525

commit v5 on v4

--- a/solution.py
+++ b/solution.py
@@ -143,7 +143,7 @@
 
     def send(c):
         def start(i, carry):
-            p = 2 * lax.rem(me // 2 + 16 + jnp.where(i % 2 == 1, (i % 16 + 1) // 2, -((i % 16) // 2)), 16) + i // 16
+            p = 4 * lax.rem(me // 4 + 8 + jnp.where(i % 2 == 1, (i % 8 + 1) // 2, -((i % 8) // 2)), 8) + lax.rem(4 - i // 8, 4)
 
             @pl.when(p != me)
             def _():

time: 42.7 us -> 42.6 us (level)
  no operation moved by 1% of the time
where the time goes in v5:
time: 42.6 us; the launch traced here: 42.2 us
  Pallas kernels  41.6 us (98%)
  between operations  0.64 us (2%)
    pallas_call x1, Pallas kernels, shards(): pl.pallas_call(kernel, out_shape=[pltpu.VMEM((8, 144, 128), F32)] * 2, in...  40.5 us
    pallas_call x1, Pallas kernels, shards(): pl.pallas_call(publish_kernel, out_shape=[jax.ShapeDtypeStruct((8, 144, 1...  1.07 us

profile of v5, /device:TPU:4, one launch (start us, length us, event | category | flops | bytes accessed | tf_op | source)
XLA Modules:
  0.0 42.2 jit_solution(12171037500059820418)
XLA Ops:
  0.6 40.5 %update.1 = (f32[8,144,128]{2,1,0:T(8,128)S(1)}, f32[8,144,128]{2,1,0:T(8,128)S(1)}) custom-call(f32[8,144,128]{2,1,0:T(8,128)} %bitcast.30, f32[8,144,128]{2,1,0:T(8,128)} %bitcast.31, f32[8,144,128]{2,1,0:T(8,128)} %bitcast.32, f32[8,144,128]{2,1,0:T(8,128)} %bitcast.33, bf16[512,256]{1,0:T(8,128)(2,1)} %constant.8.clone.fh_hbm, ...), custom_call_target="tpu_custom_call" | custom-call | tf_op jit(solution)/shard_map/update/pallas_call | solution.py:492
  41.1 1.1 %publish.1 = (f32[8,144,128]{2,1,0:T(8,128)}, f32[8,144,128]{2,1,0:T(8,128)}) custom-call(f32[8,144,128]{2,1,0:T(8,128)S(1)} %get-tuple-element.6.a, f32[8,144,128]{2,1,0:T(8,128)S(1)} %get-tuple-element.7.b), custom_call_target="tpu_custom_call" | custom-call | tf_op jit(solution)/shard_map/publish/pallas_call | solution.py:525

commit v6 on v5

--- a/solution.py
+++ b/solution.py
@@ -409,7 +409,6 @@
             down_part(half).start()
 
     to_matrices(0)
-    add_terms(0, ((0, 0, True), (4, 20, True)))
     for half in range(2):
         whole(sg.at[1, pl.ds(18 * half, 18)], sig_sem.at[1, half]).wait()
 
@@ -417,6 +416,7 @@
         def _(half=half):
             up_part(half).start()
 
+    add_terms(0, ((0, 0, True), (4, 20, True)))
     to_matrices(1)
     add_terms(4, ((4, 4, False), (0, 8, False)))
 

time: 42.6 us -> 42.6 us (level)
  no operation moved by 1% of the time
where the time goes in v6:
time: 42.6 us; the launch traced here: 42.2 us
  Pallas kernels  41.6 us (98%)
  between operations  0.64 us (2%)
    pallas_call x1, Pallas kernels, shards(): pl.pallas_call(kernel, out_shape=[pltpu.VMEM((8, 144, 128), F32)] * 2, in...  40.5 us
    pallas_call x1, Pallas kernels, shards(): pl.pallas_call(publish_kernel, out_shape=[jax.ShapeDtypeStruct((8, 144, 1...  1.07 us

profile of v6, /device:TPU:4, one launch (start us, length us, event | category | flops | bytes accessed | tf_op | source)
XLA Modules:
  0.0 42.2 jit_solution(12448437324353707460)
XLA Ops:
  0.6 40.5 %update.1 = (f32[8,144,128]{2,1,0:T(8,128)S(1)}, f32[8,144,128]{2,1,0:T(8,128)S(1)}) custom-call(f32[8,144,128]{2,1,0:T(8,128)} %bitcast.30, f32[8,144,128]{2,1,0:T(8,128)} %bitcast.31, f32[8,144,128]{2,1,0:T(8,128)} %bitcast.32, f32[8,144,128]{2,1,0:T(8,128)} %bitcast.33, bf16[512,256]{1,0:T(8,128)(2,1)} %constant.8.clone.fh_hbm, ...), custom_call_target="tpu_custom_call" | custom-call | tf_op jit(solution)/shard_map/update/pallas_call | solution.py:492
  41.1 1.1 %publish.1 = (f32[8,144,128]{2,1,0:T(8,128)}, f32[8,144,128]{2,1,0:T(8,128)}) custom-call(f32[8,144,128]{2,1,0:T(8,128)S(1)} %get-tuple-element.6.a, f32[8,144,128]{2,1,0:T(8,128)S(1)} %get-tuple-element.7.b), custom_call_target="tpu_custom_call" | custom-call | tf_op jit(solution)/shard_map/publish/pallas_call | solution.py:525
